TPU v7x, 256 devices: a whole 4x4x8 slice. The times are simulated.
256 devices in a mesh: gx: 16 (over x, y), gy: 16 (over z, core).
Axes of the slice: x: 4, y: 4, z: 8, core: 2. Of those that a mesh axis runs over, the one named last changes fastest.
Arguments:
- surface: float32 [3, 1920, 2048], P(None, 'gy', 'gx'), may hold values from -5 to 5
- depth: float32 [1920, 2048], P('gy', 'gx'), may hold values from 0.05 to 0.4
- coriolis: float32 [1920, 2048], P('gy', 'gx'), may hold values from -0.3 to 0.3
- land_sea: int32 [1920, 2048], P('gy', 'gx'), may hold values 0 or 1
- basis: bfloat16 [64, 3, 1920, 2048], P(None, None, 'gy', 'gx'), may hold values from -8 to 8
- energies: float32 [64], replicated, may hold values from 0.5 to 2
- start: float32 [68, 64], replicated, may hold values from -6 to 6
Outputs:
- final_state: float32 [3, 1920, 2048], P(None, 'gy', 'gx')
- projected: bfloat16 [64, 3, 1920, 2048], P(None, None, 'gy', 'gx')
All inputs are finite; a program needn't handle non-finite values. No bound on the sum of `land_sea` on one device may be relied on, other than what follows from the above.
Results may differ from a plain program's by a relative error of at most 0.0049.
Values sent between devices are 32-bit elements; how exact they have to be, the bound alone decides.
No kernel may reach another device: no remote copies, remote signals or barrier semaphores. Data moves between devices by JAX's collectives and lax.ppermute only.
A program may use at most 128 MiB of HBM per device.

v0:
```python
import jax
import jax.numpy as jnp
from jax import lax
from jax.experimental import pallas as pl
from jax.experimental.pallas import tpu as pltpu
from jax.sharding import PartitionSpec as P

RANK = 64
SNAPS = 4
STEPS = 8
SUBITER = 6
KCOLS = RANK + SNAPS
FIELDS = 6
WIDE = 9
PITCH = 21
HALO = 8
VMEM_LIMIT = 20 * 1024 * 1024


def pack_lane(shape, field):
    lane = lax.broadcasted_iota(jnp.int32, shape, 1)
    return (lane + (WIDE - PITCH * field) % 128) & 127


def pack_kernel(fields, packed):
    total = jnp.zeros(packed.shape, jnp.float32)
    for field in range(FIELDS):
        value = fields[field]
        if field:
            value = pltpu.roll(value, PITCH * field, 1)
        total = jnp.where(pack_lane(packed.shape, field) < 2 * WIDE, value, total)
    packed[...] = total


def crossed(eight):
    eight = list(eight)
    row = lax.broadcasted_iota(jnp.int32, eight[0].shape, 1)
    for step in (4, 2, 1):
        keep = (row & step) == 0
        for i in range(8):
            if i & step == 0:
                low, high = eight[i], eight[i + step]
                eight[i] = jnp.where(keep, low, pltpu.roll(high, step, 1))
                eight[i + step] = jnp.where(keep, pltpu.roll(low, 8 - step, 1), high)
    return eight


def seen_kernel(value, seen):
    seen[...] = jnp.zeros(seen.shape, jnp.float32)


def seen_by_kernel(value, limit=VMEM_LIMIT):
    return pl.pallas_call(
        seen_kernel,
        in_specs=[pl.BlockSpec(memory_space=pl.ANY)],
        out_shape=jax.ShapeDtypeStruct((HALO, 128), jnp.float32),
        compiler_params=pltpu.CompilerParams(vmem_limit_bytes=limit),
    )(value)


def rows_of(ref, first):
    return jnp.concatenate([ref[first + i] for i in range(8)], axis=1)


def over_lanes(left, right):
    return lax.dot_general(left, right, (((1,), (1,)), ((), ())), preferred_element_type=jnp.float32)


def combined(first, second, odd):
    west = pack_lane(first.shape, 0) < WIDE
    for field in range(1, FIELDS):
        west = west | (pack_lane(first.shape, field) < WIDE)
    return jnp.where(west == (odd == 0), second, first)


def odd_of(axis):
    return lax.axis_index(axis) & 1


def rows_kernel(fields_low, first_low, second_low, fields_high, first_high, second_high, send_first, send_second):
    odd = odd_of("gx")
    halo_low = combined(first_low[...], second_low[...], odd)
    to_south = [fields_low[field, :HALO] for field in range(FIELDS)]
    to_south += [halo_low[:HALO], fields_low[FIELDS - 1, HALO:], halo_low[HALO:]]
    to_south += [jnp.ones((HALO, 128), jnp.float32)]
    to_north = [fields_high[field] for field in range(FIELDS)]
    to_north += [combined(first_high[...], second_high[...], odd)]
    to_north += [jnp.zeros((HALO, 128), jnp.float32)] * (len(to_south) - len(to_north))
    upper = odd_of("gy") == 1
    for index, (south, north) in enumerate(zip(to_south, to_north)):
        span = slice(index * HALO, (index + 1) * HALO)
        send_first[span, :] = jnp.where(upper, south, north)
        send_second[span, :] = jnp.where(upper, north, south)


def window_kernel(
    fields, first_side, second_side, first_rows, second_rows, *rest
):
    turned, gram, _, _, state, snaps, sums, height, zonal, merid, statics, frames = rest
    rows = fields.shape[1]
    tall = rows + 2 * HALO
    upper = odd_of("gy") == 1
    from_north = jnp.where(upper, second_rows[...], first_rows[...])
    from_south = jnp.where(upper, first_rows[...], second_rows[...])
    halo = jnp.concatenate(
        [
            from_south[FIELDS * HALO : (FIELDS + 1) * HALO, :],
            combined(first_side[...], second_side[...], odd_of("gx")),
            from_north[FIELDS * HALO : (FIELDS + 1) * HALO, :],
        ],
        axis=0,
    )

    def extended(field, value):
        span = slice(field * HALO, (field + 1) * HALO)
        main = jnp.concatenate([from_south[span, :], value, from_north[span, :]], axis=0)
        side = pltpu.roll(halo, 128 - PITCH * field, 1) if field else halo
        return jnp.concatenate([main, side], axis=1)

    def east(value):
        return pltpu.roll(value, 255, 1)

    def west(value):
        return pltpu.roll(value, 1, 1)

    def north(value):
        return pltpu.roll(value, tall - 1, 0)

    values = [fields[field] for field in range(FIELDS)]
    for ref, field in ((height, 0), (zonal, 1), (merid, 2)):
        ref[...] = extended(field, values[field])
    statics[0] = extended(3, values[3])
    wet = extended(4, values[4])
    statics[1] = wet * east(wet)
    statics[2] = wet * north(wet)
    deep = extended(5, values[5])
    statics[3] = 0.5 * (deep + east(deep))
    side = pltpu.roll(from_north[(FIELDS + 2) * HALO : (FIELDS + 3) * HALO, :], 128 - PITCH * 5, 1)
    above = jnp.concatenate([from_north[(FIELDS + 1) * HALO : (FIELDS + 2) * HALO, :], side], axis=1)
    last = lax.broadcasted_iota(jnp.int32, (tall, 256), 0) == tall - 1
    upper = jnp.where(last, above[:1], north(deep))
    statics[4] = 0.5 * (deep + upper)
    there = from_north[(FIELDS + 3) * HALO :, :]
    there = jnp.concatenate([there, there], axis=1)
    row = lax.broadcasted_iota(jnp.int32, (8, 256), 0)

    def one_step():
        def shifted_south(value, below):
            return jnp.where(row == 0, pltpu.roll(below, 1, 0), pltpu.roll(value, 1, 0))

        def shifted_north(value, above):
            return jnp.where(row == 7, pltpu.roll(above, 7, 0), pltpu.roll(value, 7, 0))

        before = None
        for first in range(0, tall, 8):
            span = slice(first, first + 8)
            flow, across = zonal[span, :], merid[span, :]
            flux = statics[3, span, :] * flow
            drop = statics[4, span, :] * across
            sums = across + east(across)
            low = before or dict(drop=drop, sums=sums)
            high = height[span, :] - (flux - west(flux)) - (drop - shifted_south(drop, low["drop"]))
            if first == tall - HALO:
                high = high * there
            vbar = 0.25 * (sums + shifted_south(sums, low["sums"]))
            flow = statics[1, span, :] * (flow - (east(high) - high) + statics[0, span, :] * vbar)
            height[span, :] = high
            zonal[span, :] = flow
            now = dict(drop=drop, sums=sums, high=high, pairs=flow + west(flow), across=across, span=span)
            if before:
                finish_merid(before, now["high"], now["pairs"], shifted_north)
            before = now
        finish_merid(before, before["high"], before["pairs"], shifted_north)

    def finish_merid(rows_here, high_above, pairs_above, shifted_north):
        high, pairs_here, span = rows_here["high"], rows_here["pairs"], rows_here["span"]
        ubar = 0.25 * (pairs_here + shifted_north(pairs_here, pairs_above))
        slope = shifted_north(high, high_above) - high
        merid[span, :] = statics[2, span, :] * (rows_here["across"] - slope - statics[0, span, :] * ubar)

    def some_steps(turn, carry):
        for _ in range(STEPS // SNAPS):
            one_step()
        for index, ref in enumerate((height, zonal, merid)):
            place = pl.ds(index * rows * 8 + turn, rows, stride=8)
            frames[place, :] = ref[HALO : HALO + rows, :128]
        return carry

    frames[...] = jnp.zeros(frames.shape, jnp.float32)

    lax.fori_loop(0, SNAPS, some_steps, 0)
    for index, ref in enumerate((height, zonal, merid)):
        state[index] = ref[HALO : HALO + rows, :128]
    snaps[...] = frames[...].reshape(snaps.shape).astype(jnp.bfloat16)

    total = jnp.zeros((8, RANK + 8), jnp.float32)
    for field in range(3):
        for first in range(0, rows, 8):
            frame = rows_of(snaps, field * rows + first)
            tile = jnp.concatenate([rows_of(turned, field * rows + first), frame], axis=0)
            total = total + over_lanes(frame, tile)
    pack_sums(gram[...], total, sums)


def triangle(shape):
    row, lane = (lax.broadcasted_iota(jnp.int32, shape, axis) for axis in (0, 1))
    return lane - shape[0] - row, (lane >= shape[0]) & (lane < 2 * shape[0])


def pack_sums(gram, cross, sums):
    half = RANK // 2
    wide = jnp.concatenate([gram, jnp.zeros((RANK, RANK), jnp.float32)], axis=1)
    apart, there = triangle((half, 128))
    first = pltpu.roll(wide[:half], half, 1)
    block = jnp.where(there, jnp.where(apart >= 0, first, wide[half:]), pltpu.roll(first, RANK, 1))
    block = jnp.where(there | (apart < 0), block, 0.0)
    sums[: half // 2, :] = block[: half // 2] + pltpu.roll(block[half // 2 :], RANK, 1)
    diagonal = jnp.sum(jnp.where(there & (apart == 0), wide[half:], 0.0), axis=0, keepdims=True)
    cross = jnp.concatenate([cross, jnp.zeros((8, 128 - RANK - 8), jnp.float32)], axis=1)
    row = lax.broadcasted_iota(jnp.int32, cross.shape, 0)
    sums[half // 2 :, :] = jnp.where(row < SNAPS, cross, jnp.where(row == SNAPS, diagonal, 0.0))


def unpacked(sums):
    half = RANK // 2
    upper = sums[: half // 2]
    block = jnp.concatenate([upper, pltpu.roll(upper, RANK, 1)], axis=0)
    lane = lax.broadcasted_iota(jnp.int32, block.shape, 1)
    apart, there = triangle(block.shape)
    rest = sums[half // 2 :]
    first = jnp.where(there, jnp.where(apart > 0, block, jnp.where(apart == 0, 0.5 * block, 0.0)), 0.0)
    first = pltpu.roll(first, 128 - half, 1) + jnp.where(there, pltpu.roll(block, half, 1), 0.0)
    diagonal = jnp.where(there & (apart == 0), 0.5 * rest[SNAPS : SNAPS + 1], 0.0)
    second = jnp.where(there & (apart < 0), block, diagonal)
    row = lax.broadcasted_iota(jnp.int32, rest.shape, 0)
    lane = lax.broadcasted_iota(jnp.int32, rest.shape, 1)
    third = jnp.where(row < SNAPS, jnp.where(lane < RANK, rest, 0.5 * rest), 0.0)
    third = jnp.where(lane < KCOLS, third, 0.0)
    beyond = jnp.zeros((128 - RANK - 8, 128), jnp.float32)
    matrix = jnp.concatenate([first, second, third, beyond], axis=0)
    return matrix + jnp.transpose(matrix, (1, 0))


def pairs(offset, around):
    partners = [(i, (((i - offset) ^ 1) + offset) % 16) for i in range(16)]
    return [(i, j) for i, j in partners if around or abs(i - j) == 1]


def window(surface, depth, coriolis, land_sea, basis):
    rows, cols = depth.shape
    whole = pltpu.CompilerParams(vmem_limit_bytes=VMEM_LIMIT)
    fields = jnp.pad(surface, ((0, FIELDS - 3), (0, 0), (0, 0)))
    for field, value in ((3, coriolis), (4, land_sea), (5, depth)):
        around = ((field, FIELDS - 1 - field), (0, 0), (0, 0))
        fields = fields + jnp.pad(value[None], around).astype(jnp.float32)
    packed = pl.pallas_call(
        pack_kernel,
        out_shape=jax.ShapeDtypeStruct((rows, cols), jnp.float32),
        compiler_params=whole,
    )(fields)
    basis, packed = lax.optimization_barrier((basis, packed))
    sides = [lax.ppermute(packed, "gx", pairs(offset, True)) for offset in (0, 1)]

    early = seen_by_kernel(basis, 55 * 1024 * 1024)
    early, sides[0] = lax.optimization_barrier((early, sides[0]))
    basis, early = lax.optimization_barrier((basis, early))
    late = seen_by_kernel(basis)
    basis, late = lax.optimization_barrier((basis, late))
    turned = jnp.transpose(basis, (1, 2, 0, 3)).reshape(3 * rows, RANK, cols)
    turned, sides[1], late = lax.optimization_barrier((turned, sides[1], late))

    def strips(height, index):
        side = pl.BlockSpec((height, cols), lambda i: (index, 0))
        return [pl.BlockSpec((FIELDS, height, cols), lambda i: (0, index, 0)), side, side]

    slab = jax.ShapeDtypeStruct(((FIELDS + 4) * HALO, cols), jnp.float32)
    sends = pl.pallas_call(
        rows_kernel,
        grid=(1,),
        in_specs=strips(2 * HALO, 0) + strips(HALO, rows // HALO - 1),
        out_shape=(slab, slab),
        compiler_params=whole,
    )(fields, *sides, fields, *sides)
    slabs = [lax.ppermute(send, "gy", pairs(offset, False)) for offset, send in enumerate(sends)]
    turned, slabs[0] = lax.optimization_barrier((turned, slabs[0]))
    gram = lax.dot_general(
        turned, turned, (((0, 2), (0, 2)), ((), ())), preferred_element_type=jnp.float32
    )
    gram, slabs = lax.optimization_barrier((gram, slabs))
    tall = (rows + 2 * HALO, 2 * cols)
    final_state, snaps, sums = pl.pallas_call(
        window_kernel,
        out_shape=(
            jax.ShapeDtypeStruct((3, rows, cols), jnp.float32),
            jax.ShapeDtypeStruct((3 * rows, 8, cols), jnp.bfloat16),
            jax.ShapeDtypeStruct((RANK // 4 + 8, 128), jnp.float32),
        ),
        scratch_shapes=[pltpu.VMEM(tall, jnp.float32)] * 3
        + [pltpu.VMEM((5,) + tall, jnp.float32), pltpu.VMEM((3 * rows * 8, cols), jnp.float32)],
        compiler_params=whole,
    )(fields, *sides, *slabs, turned, gram, early, late)
    return final_state, snaps, turned, sums


def exchanged(value, axis, partner):
    return lax.ppermute(value, axis, [(i, partner(i)) for i in range(16)])


def quad_sum(value, axis, one, two):
    first = exchanged(value, axis, lambda i: i ^ one)
    second = exchanged(value, axis, lambda i: i ^ two)
    third = exchanged(value, axis, lambda i: i ^ one ^ two)
    return (value + first) + (second + third)


def total_over_devices(value):
    value = quad_sum(value, "gy", 1, 2)
    ring = lambda a: ((a - 1) ^ 1) + 1 if 0 < a < 7 else 7 - a
    value = value + exchanged(value, "gy", lambda i: ring(i // 2) * 2 + i % 2)
    ring = lambda a: (7 - a) if a in (1, 2, 5, 6) else {0: 3, 3: 0, 4: 7, 7: 4}[a]
    value = value + exchanged(value, "gy", lambda i: ring(i // 2) * 2 + i % 2)
    value = quad_sum(value, "gx", 1, 4)
    return quad_sum(value, "gx", 3, 12)


ORDERS = ((0, 0), (0, 1), (1, 0), (0, 2), (1, 1), (2, 0))
PITCH_OF_SWEEP = 176
LEAD = 56
GROUPS = ((0, 32), (32, 32))


def parts_of(value):
    parts = []
    for _ in range(3):
        parts.append(value.astype(jnp.bfloat16))
        value = value - parts[-1].astype(jnp.float32)
    return parts


def parts_dot(left, right, count, turned=False):
    left = jnp.concatenate([left[i] for i, _ in ORDERS[:count]], axis=1)
    right = jnp.concatenate([right[j] for _, j in ORDERS[:count]], axis=1 if turned else 0)
    return lax.dot_general(
        left, right, (((1,), (1 if turned else 0,)), ((), ())), preferred_element_type=jnp.float32
    )


def refine(gram, start, store):
    blocks = RANK // 8
    sweep = lax.broadcasted_iota(jnp.int32, (8, 128), 0)
    gram = parts_of(gram)
    made = None
    for time in range(blocks + SUBITER - 1):
        inputs = []
        for i in range(8):
            value = jnp.zeros((8, 128), jnp.float32) if made is None else pltpu.roll(made[i], 1, 0)
            if time < blocks:
                value = jnp.where(sweep == 0, start[8 * time + i : 8 * time + i + 1, :], value)
            inputs.append(value)
        active = (sweep <= time) & (sweep > time - blocks) & (sweep < SUBITER)
        images = parts_dot(parts_of(jnp.concatenate(inputs, axis=0)), gram, 6)
        running = [k for k in range(SUBITER) if 0 < time - k < blocks]
        if running:
            history = [store[pl.ds(k * PITCH_OF_SWEEP + LEAD, 8 * (time - k)), :] for k in running]
            length = sum(rows.shape[0] for rows in history)
            if length % 128:
                history.append(jnp.zeros((128 - length % 128, 128), jnp.float32))
            history = parts_of(jnp.concatenate(history, axis=0))
            inner = parts_dot(parts_of(images), history, 3, turned=True)
            row = lax.broadcasted_iota(jnp.int32, inner.shape, 0) & 7
            col = lax.broadcasted_iota(jnp.int32, inner.shape, 1)
            owner, edge = jnp.full(inner.shape, running[0], jnp.int32), 0
            for k in running[:-1]:
                edge += 8 * (time - k)
                owner = owner + jnp.where(col >= edge, 1, 0)
            inner = jnp.where(row == owner, inner, 0.0)
            images = images - parts_dot(parts_of(inner), history, 5)
        parts = [images[8 * i : 8 * i + 8] for i in range(8)]
        square = {
            (i, j): jnp.sum(parts[i] * parts[j], axis=1, keepdims=True)
            for i in range(8)
            for j in range(i, 8)
        }
        made = []
        for i in range(8):
            scale = lax.rsqrt(square[i, i])
            unit = parts[i] * scale
            made.append(jnp.where(active, unit, 0.0))
            lower = {j: square[i, j] * scale for j in range(i + 1, 8)}
            for j in range(i + 1, 8):
                parts[j] = parts[j] - lower[j] * unit
                for p in range(j, 8):
                    square[j, p] = square[j, p] - lower[j] * lower[p]
        for i in range(8):
            store[pl.ds(LEAD + 8 * time + i, 8, stride=PITCH_OF_SWEEP - 8), :] = made[i]
        yield time


def finish_kernel(
    sums, outer, start, weights, snaps, turned, projected, out, store, store_sems
):
    rows = out.shape[2]
    stores = [
        [
            pltpu.make_async_copy(
                out.at[pl.ds(first, size), f], projected.at[pl.ds(first, size), f], store_sems.at[3 * index + f]
            )
            for f in range(3)
        ]
        for index, (first, size) in enumerate(GROUPS)
    ]
    bands = [(f, first, min(16, rows - first)) for f in range(3) for first in range(0, rows, 16)]
    gram = unpacked(sums[...])

    def mix_of(index):
        first, size = GROUPS[index]
        rows_of_mix = store[pl.ds((SUBITER - 1) * PITCH_OF_SWEEP + LEAD + first, size), :] * weights[...]
        return rows_of_mix[:, : RANK + 8].astype(jnp.bfloat16)

    def mixed(index, mix, field, first, count):
        made, size = GROUPS[index]
        done = []
        for h in range(count // 8):
            spot = field * rows + first + 8 * h
            tile = jnp.concatenate([rows_of(turned, spot), rows_of(snaps, spot)], axis=0)
            total = jnp.dot(mix, tile, preferred_element_type=jnp.float32)
            parts = [total[:, 128 * i : 128 * i + 128].reshape(size // 8, 8, 128) for i in range(8)]
            done.append(jnp.stack(crossed(parts), axis=1).reshape(size, 8, 128))
        done = done[0] if count == 8 else jnp.concatenate(done, axis=1)
        out[made : made + size, field, first : first + count, :] = done.astype(jnp.bfloat16)
        if first + count == rows:
            stores[index][field].start()

    last = RANK // 8 + SUBITER - 2
    ready = [SUBITER - 2 + (first + size) // 8 for first, size in GROUPS]
    work = []
    for time in refine(gram * outer[...], start, store):
        for index, due in enumerate(ready):
            if time == due:
                mix = mix_of(index)
                work += [(index, mix, *band) for band in bands]
        if time < last:
            until = min([due for due in ready if due > time])
            now = -(-len(work) // (until - time))
            for item in work[:now]:
                mixed(*item)
            work = work[now:]
    for item in work:
        mixed(*item)
    for group in stores:
        for copy in group:
            copy.wait()


def local(surface, depth, coriolis, land_sea, basis, energies, start):
    rows, cols = depth.shape
    final_state, snaps, turned, sums = window(surface, depth, coriolis, land_sea, basis)
    sums = total_over_devices(sums)
    cells = 3.0 * rows * cols * lax.axis_size("gx") * lax.axis_size("gy")
    weights = jnp.concatenate([energies, jnp.ones((SNAPS,), jnp.float32)])
    weights = jnp.pad(weights, (0, 128 - KCOLS))
    outer = weights[:, None] * weights[None, :] / cells
    begin = jnp.pad(start.T, ((0, 0), (0, 128 - KCOLS)))
    vmem = pl.BlockSpec(memory_space=pltpu.VMEM)
    projected = pl.pallas_call(
        finish_kernel,
        in_specs=[vmem] * 6,
        out_specs=pl.BlockSpec(memory_space=pl.ANY),
        out_shape=jax.ShapeDtypeStruct(basis.shape, jnp.bfloat16),
        scratch_shapes=[
            pltpu.VMEM(basis.shape, jnp.bfloat16),
            pltpu.VMEM((8 * PITCH_OF_SWEEP, 128), jnp.float32),
            pltpu.SemaphoreType.DMA((3 * len(GROUPS),)),
        ],
        compiler_params=pltpu.CompilerParams(vmem_limit_bytes=VMEM_LIMIT),
    )(sums, outer, begin, weights[None, :], snaps, turned)
    return (final_state, projected)


def solution(mesh):
    placed = (
        P(None, "gy", "gx"),
        P("gy", "gx"),
        P("gy", "gx"),
        P("gy", "gx"),
        P(None, None, "gy", "gx"),
        P(),
        P(),
    )
    return jax.shard_map(
        local,
        mesh=mesh,
        in_specs=placed,
        out_specs=(P(None, "gy", "gx"), P(None, None, "gy", "gx")),
        check_vma=False,
    )
```

profile of v0, /device:TPU:6, one launch (start us, length us, event | category | flops | bytes accessed | tf_op | source)
XLA Modules:
  0.0 65.9 jit_solution(11573059630599641391)
XLA Ops:
  0.6 0.0 copy-start
  0.6 1.2 %pad_add_fusion.fields.fields_low.fields_high = f32[6,120,128]{2,1,0:T(8,128)S(1)} fusion(f32[1,120,128]{2,1,0:T(8,128)} %bitcast.16, s32[1,120,128]{2,1,0:T(8,128)} %bitcast.17, f32[1,120,128]{2,1,0:T(8,128)} %bitcast.18, f32[3,120,128]{2,1,0:T(8,128)} %param.7), kind=kLoop, calls=%fused_computation.1 | loop fusion | flops 368640 | bytes 737280 | tf_op jit(solution)/shard_map/add | solution.py:255
  1.8 0.1 shard_map.86
  2.0 1.7 %collective-permute-start = (f32[120,128]{1,0:T(8,128)S(1)}, f32[120,128]{1,0:T(8,128)S(1)}, u32[]{:S(2)}, u32[]{:S(2)}) collective-permute-start(f32[120,128]{1,0:T(8,128)S(1)} %shard_map.86), channel_id=1, source_target_pairs={{0,16},{16,0},{32,48},{48,32},{64,80},{80,64},{96,112},{112,96},{1... | collective-permute-start | bytes 184328 | tf_op jit(solution)/shard_map/ppermute | solution.py:262
  3.6 2.4 %collective-permute-start.1 = (f32[120,128]{1,0:T(8,128)S(1)}, f32[120,128]{1,0:T(8,128)S(1)}, u32[]{:S(2)}, u32[]{:S(2)}) collective-permute-start(f32[120,128]{1,0:T(8,128)S(1)} %shard_map.86), channel_id=1, source_target_pairs={{0,240},{16,32},{32,16},{48,64},{64,48},{80,96},{96,80},{112,128},... | collective-permute-start | bytes 184328 | tf_op jit(solution)/shard_map/ppermute | solution.py:262
  6.1 0.6 shard_map.87.rest_2_
  6.7 0.0 collective-permute-done.first_low.first_high.first_side
  6.7 0.0 copy-done
  6.7 1.6 %copy.9 = bf16[3,120,64,128]{3,2,1,0:T(8,128)(2,1)S(1)} copy(bf16[3,120,64,128]{3,1,0,2:T(8,128)(2,1)S(1)} %bitcast.15) | data formatting | bytes 11796480 | tf_op jit(solution)/shard_map/transpose | solution.py:269
  8.3 1.7 %collective-permute-done.1.second_low.second_high.second_side = f32[120,128]{1,0:T(8,128)S(1)} collective-permute-done((f32[120,128]{1,0:T(8,128)S(1)}, f32[120,128]{1,0:T(8,128)S(1)}, u32[]{:S(2)}, u32[]{:S(2)}) %collective-permute-start.1) | collective-permute-done | bytes 61472 | tf_op jit(solution)/shard_map/ppermute | solution.py:262
  10.0 0.1 collective-permute-start.2
  10.1 0.0 copy-start.1
  10.1 0.7 %collective-permute-start.3 = (f32[80,128]{1,0:T(8,128)S(1)}, f32[80,128]{1,0:T(8,128)S(1)}, u32[]{:S(2)}, u32[]{:S(2)}) collective-permute-start(f32[80,128]{1,0:T(8,128)S(1)} %get-tuple-element.35), channel_id=1, source_target_pairs={{1,2},{2,1},{3,4},{4,3},{5,6},{6,5},{7,8},{8,7},{9,10},{10,9},{11,... | collective-permute-start | bytes 122888 | tf_op jit(solution)/shard_map/ppermute | solution.py:284
  10.8 0.5 collective-permute-done.2.first_rows
  11.3 1.7 %convolution_bitcast_fusion.rest_1_ = f32[64,64]{1,0:T(8,128)S(1)} fusion(bf16[360,64,128]{2,1,0:T(8,128)(2,1)S(1)} %bitcast.12), kind=kOutput, calls=%fused_computation | convolution fusion | flops 377487360 | bytes 5914624 | tf_op jit(solution)/shard_map/dot_general | solution.py:286
  13.0 0.0 copy-start.3
  13.0 0.0 copy-start.2
  13.0 0.0 collective-permute-done.3.second_rows
  13.0 0.0 copy-done.1
  13.0 5.0 %shard_map.90 = (f32[3,120,128]{2,1,0:T(8,128)}, bf16[360,8,128]{2,1,0:T(8,128)(2,1)S(1)}, f32[24,128]{1,0:T(8,128)S(1)}) custom-call(f32[6,120,128]{2,1,0:T(8,128)S(1)} %pad_add_fusion.fields.fields_low.fields_high, f32[120,128]{1,0:T(8,128)S(1)} %collective-permute-done.first_low.first_high.first_side, ...), custom_call_target="tpu_custom_call" | custom-call | tf_op jit(solution)/shard_map/pallas_call | solution.py:291
  18.1 4.5 %collective-permute-start.6 = (f32[24,128]{1,0:T(8,128)S(1)}, f32[24,128]{1,0:T(8,128)S(1)}, u32[]{:S(2)}, u32[]{:S(2)}) collective-permute-start(f32[24,128]{1,0:T(8,128)S(1)} %get-tuple-element.42), channel_id=1, source_target_pairs={{0,3},{1,2},{2,1},{3,0},{4,7},{5,6},{6,5},{7,4},{8,11},{9,10},{10,... | collective-permute-start | bytes 36872 | tf_op jit(solution)/shard_map/ppermute | solution.py:306
  22.6 0.1 collective-permute-start.5
  22.7 0.0 collective-permute-start.4
  22.7 1.3 %collective-permute-done.6 = f32[24,128]{1,0:T(8,128)S(1)} collective-permute-done((f32[24,128]{1,0:T(8,128)S(1)}, f32[24,128]{1,0:T(8,128)S(1)}, u32[]{:S(2)}, u32[]{:S(2)}) %collective-permute-start.6) | collective-permute-done | bytes 12320 | tf_op jit(solution)/shard_map/ppermute | solution.py:306
  24.0 2.3 %collective-permute-done.5 = f32[24,128]{1,0:T(8,128)S(1)} collective-permute-done((f32[24,128]{1,0:T(8,128)S(1)}, f32[24,128]{1,0:T(8,128)S(1)}, u32[]{:S(2)}, u32[]{:S(2)}) %collective-permute-start.5) | collective-permute-done | bytes 12320 | tf_op jit(solution)/shard_map/ppermute | solution.py:306
  26.3 0.0 collective-permute-done.4
  26.3 5.0 %collective-permute-start.7 = (f32[24,128]{1,0:T(8,128)S(1)}, f32[24,128]{1,0:T(8,128)S(1)}, u32[]{:S(2)}, u32[]{:S(2)}) collective-permute-start(f32[24,128]{1,0:T(8,128)S(1)} %add_add_fusion.2), channel_id=1, source_target_pairs={{0,14},{1,15},{2,4},{3,5},{4,2},{5,3},{6,8},{7,9},{8,6},{9,7},{10,... | collective-permute-start | bytes 36872 | tf_op jit(solution)/shard_map/ppermute | solution.py:306
  31.3 1.7 %collective-permute-done.7 = f32[24,128]{1,0:T(8,128)S(1)} collective-permute-done((f32[24,128]{1,0:T(8,128)S(1)}, f32[24,128]{1,0:T(8,128)S(1)}, u32[]{:S(2)}, u32[]{:S(2)}) %collective-permute-start.7) | collective-permute-done | bytes 12320 | tf_op jit(solution)/shard_map/ppermute | solution.py:306
  33.0 2.3 %collective-permute-start.8 = (f32[24,128]{1,0:T(8,128)S(1)}, f32[24,128]{1,0:T(8,128)S(1)}, u32[]{:S(2)}, u32[]{:S(2)}) collective-permute-start(f32[24,128]{1,0:T(8,128)S(1)} %add.62), channel_id=1, source_target_pairs={{0,6},{1,7},{2,12},{3,13},{4,10},{5,11},{6,0},{7,1},{8,14},{9,15},... | collective-permute-start | bytes 36872 | tf_op jit(solution)/shard_map/ppermute | solution.py:306
  35.3 3.2 %collective-permute-done.8 = f32[24,128]{1,0:T(8,128)S(1)} collective-permute-done((f32[24,128]{1,0:T(8,128)S(1)}, f32[24,128]{1,0:T(8,128)S(1)}, u32[]{:S(2)}, u32[]{:S(2)}) %collective-permute-start.8) | collective-permute-done | bytes 12320 | tf_op jit(solution)/shard_map/ppermute | solution.py:306
  38.5 0.0 collective-permute-start.11
  38.5 1.0 %collective-permute-start.10 = (f32[24,128]{1,0:T(8,128)S(1)}, f32[24,128]{1,0:T(8,128)S(1)}, u32[]{:S(2)}, u32[]{:S(2)}) collective-permute-start(f32[24,128]{1,0:T(8,128)S(1)} %add.63), channel_id=1, source_target_pairs={{0,64},{16,80},{32,96},{48,112},{64,0},{80,16},{96,32},{112,48},{1... | collective-permute-start | bytes 36872 | tf_op jit(solution)/shard_map/ppermute | solution.py:306
  39.5 2.5 %collective-permute-start.9 = (f32[24,128]{1,0:T(8,128)S(1)}, f32[24,128]{1,0:T(8,128)S(1)}, u32[]{:S(2)}, u32[]{:S(2)}) collective-permute-start(f32[24,128]{1,0:T(8,128)S(1)} %add.63), channel_id=1, source_target_pairs={{0,16},{16,0},{32,48},{48,32},{64,80},{80,64},{96,112},{112,96},{1... | collective-permute-start | bytes 36872 | tf_op jit(solution)/shard_map/ppermute | solution.py:306
  42.0 0.0 copy-done.3
  42.0 1.1 %collective-permute-done.11 = f32[24,128]{1,0:T(8,128)S(1)} collective-permute-done((f32[24,128]{1,0:T(8,128)S(1)}, f32[24,128]{1,0:T(8,128)S(1)}, u32[]{:S(2)}, u32[]{:S(2)}) %collective-permute-start.11) | collective-permute-done | bytes 12320 | tf_op jit(solution)/shard_map/ppermute | solution.py:306
  43.1 0.0 collective-permute-done.10
  43.1 0.6 collective-permute-done.9
  43.7 2.1 %collective-permute-start.14 = (f32[24,128]{1,0:T(8,128)S(1)}, f32[24,128]{1,0:T(8,128)S(1)}, u32[]{:S(2)}, u32[]{:S(2)}) collective-permute-start(f32[24,128]{1,0:T(8,128)S(1)} %add_add_fusion.1), channel_id=1, source_target_pairs={{0,240},{16,224},{32,208},{48,192},{64,176},{80,160},{96,144},{112... | collective-permute-start | bytes 36872 | tf_op jit(solution)/shard_map/ppermute | solution.py:306
  45.8 3.9 %collective-permute-start.13 = (f32[24,128]{1,0:T(8,128)S(1)}, f32[24,128]{1,0:T(8,128)S(1)}, u32[]{:S(2)}, u32[]{:S(2)}) collective-permute-start(f32[24,128]{1,0:T(8,128)S(1)} %add_add_fusion.1), channel_id=1, source_target_pairs={{0,192},{16,208},{32,224},{48,240},{64,128},{80,144},{96,160},{112... | collective-permute-start | bytes 36872 | tf_op jit(solution)/shard_map/ppermute | solution.py:306
  49.7 0.0 collective-permute-start.12
  49.7 0.1 multiply_multiply_fusion.outer
  49.8 0.0 copy-done.2
  49.9 0.8 %collective-permute-done.14 = f32[24,128]{1,0:T(8,128)S(1)} collective-permute-done((f32[24,128]{1,0:T(8,128)S(1)}, f32[24,128]{1,0:T(8,128)S(1)}, u32[]{:S(2)}, u32[]{:S(2)}) %collective-permute-start.14) | collective-permute-done | bytes 12320 | tf_op jit(solution)/shard_map/ppermute | solution.py:306
  50.7 0.8 %collective-permute-done.13 = f32[24,128]{1,0:T(8,128)S(1)} collective-permute-done((f32[24,128]{1,0:T(8,128)S(1)}, f32[24,128]{1,0:T(8,128)S(1)}, u32[]{:S(2)}, u32[]{:S(2)}) %collective-permute-start.13) | collective-permute-done | bytes 12320 | tf_op jit(solution)/shard_map/ppermute | solution.py:306
  51.5 3.1 %collective-permute-done.12 = f32[24,128]{1,0:T(8,128)S(1)} collective-permute-done((f32[24,128]{1,0:T(8,128)S(1)}, f32[24,128]{1,0:T(8,128)S(1)}, u32[]{:S(2)}, u32[]{:S(2)}) %collective-permute-start.12) | collective-permute-done | bytes 12320 | tf_op jit(solution)/shard_map/ppermute | solution.py:306
  54.7 11.1 %shard_map.91 = bf16[64,3,120,128]{3,2,1,0:T(8,128)(2,1)} custom-call(f32[24,128]{1,0:T(8,128)S(1)} %add_add_fusion.sums, f32[128,128]{1,0:T(8,128)S(1)} %multiply_multiply_fusion.outer, f32[64,128]{1,0:T(8,128)S(1)} %pad.30.start, f32[1,128]{1,0:T(1,128)S(1)} %get-tuple-element.44.weights, bf16[360,8,128]{2,1,0:T(8,128)(2,1)S(1)} %get-tuple-element.43.snaps, ...), custom_call_target="tpu_custom_call" | custom-call | tf_op jit(solution)/shard_map/pallas_call | solution.py:465
  (9 shorter events, 0.1 us)
Async XLA Ops:
  0.6 6.1 %copy-start = (bf16[64,3,120,128]{3,2,1,0:T(8,128)(2,1)S(1)}, bf16[64,3,120,128]{3,2,1,0:T(8,128)(2,1)}, u32[]{:S(2)}) copy-start(bf16[64,3,120,128]{3,2,1,0:T(8,128)(2,1)} %value.1) | copy-start | bytes 17694724
  2.0 4.7 %collective-permute-start = (f32[120,128]{1,0:T(8,128)S(1)}, f32[120,128]{1,0:T(8,128)S(1)}, u32[]{:S(2)}, u32[]{:S(2)}) collective-permute-start(f32[120,128]{1,0:T(8,128)S(1)} %shard_map.86), channel_id=1, source_target_pairs={{0,16},{16,0},{32,48},{48,32},{64,80},{80,64},{96,112},{112,96},{1... | collective-permute-start | bytes 184328 | tf_op jit(solution)/shard_map/ppermute | solution.py:262
  3.6 6.3 %collective-permute-start.1 = (f32[120,128]{1,0:T(8,128)S(1)}, f32[120,128]{1,0:T(8,128)S(1)}, u32[]{:S(2)}, u32[]{:S(2)}) collective-permute-start(f32[120,128]{1,0:T(8,128)S(1)} %shard_map.86), channel_id=1, source_target_pairs={{0,240},{16,32},{32,16},{48,64},{64,48},{80,96},{96,80},{112,128},... | collective-permute-start | bytes 184328 | tf_op jit(solution)/shard_map/ppermute | solution.py:262
  10.0 1.3 %collective-permute-start.2 = (f32[80,128]{1,0:T(8,128)S(1)}, f32[80,128]{1,0:T(8,128)S(1)}, u32[]{:S(2)}, u32[]{:S(2)}) collective-permute-start(f32[80,128]{1,0:T(8,128)S(1)} %get-tuple-element.32), channel_id=1, source_target_pairs={{0,1},{1,0},{2,3},{3,2},{4,5},{5,4},{6,7},{7,6},{8,9},{9,8},{10,11... | collective-permute-start | bytes 122888 | tf_op jit(solution)/shard_map/ppermute | solution.py:284
  10.1 2.9 %copy-start.1 = (f32[8,128]{1,0:T(8,128)S(1)}, f32[8,128]{1,0:T(8,128)}, u32[]{:S(2)}) copy-start(f32[8,128]{1,0:T(8,128)} %shard_map.87.rest_2_) | copy-start | bytes 12292
  10.1 2.9 %collective-permute-start.3 = (f32[80,128]{1,0:T(8,128)S(1)}, f32[80,128]{1,0:T(8,128)S(1)}, u32[]{:S(2)}, u32[]{:S(2)}) collective-permute-start(f32[80,128]{1,0:T(8,128)S(1)} %get-tuple-element.35), channel_id=1, source_target_pairs={{1,2},{2,1},{3,4},{4,3},{5,6},{6,5},{7,8},{8,7},{9,10},{10,9},{11,... | collective-permute-start | bytes 122888 | tf_op jit(solution)/shard_map/ppermute | solution.py:284
  13.0 29.0 %copy-start.3 = (f32[64]{0:T(128)S(1)}, f32[64]{0:T(128)}, u32[]{:S(2)}) copy-start(f32[64]{0:T(128)} %param.12) | copy-start | bytes 772
  13.0 36.9 %copy-start.2 = (f32[68,64]{0,1:T(8,128)S(1)}, f32[68,64]{0,1:T(8,128)}, u32[]{:S(2)}) copy-start(f32[68,64]{0,1:T(8,128)} %param.13) | copy-start | bytes 52228
  18.1 6.0 %collective-permute-start.6 = (f32[24,128]{1,0:T(8,128)S(1)}, f32[24,128]{1,0:T(8,128)S(1)}, u32[]{:S(2)}, u32[]{:S(2)}) collective-permute-start(f32[24,128]{1,0:T(8,128)S(1)} %get-tuple-element.42), channel_id=1, source_target_pairs={{0,3},{1,2},{2,1},{3,0},{4,7},{5,6},{6,5},{7,4},{8,11},{9,10},{10,... | collective-permute-start | bytes 36872 | tf_op jit(solution)/shard_map/ppermute | solution.py:306
  22.6 3.7 %collective-permute-start.5 = (f32[24,128]{1,0:T(8,128)S(1)}, f32[24,128]{1,0:T(8,128)S(1)}, u32[]{:S(2)}, u32[]{:S(2)}) collective-permute-start(f32[24,128]{1,0:T(8,128)S(1)} %get-tuple-element.42), channel_id=1, source_target_pairs={{0,2},{1,3},{2,0},{3,1},{4,6},{5,7},{6,4},{7,5},{8,10},{9,11},{10,... | collective-permute-start | bytes 36872 | tf_op jit(solution)/shard_map/ppermute | solution.py:306
  22.7 3.6 %collective-permute-start.4 = (f32[24,128]{1,0:T(8,128)S(1)}, f32[24,128]{1,0:T(8,128)S(1)}, u32[]{:S(2)}, u32[]{:S(2)}) collective-permute-start(f32[24,128]{1,0:T(8,128)S(1)} %get-tuple-element.42), channel_id=1, source_target_pairs={{0,1},{1,0},{2,3},{3,2},{4,5},{5,4},{6,7},{7,6},{8,9},{9,8},{10,11... | collective-permute-start | bytes 36872 | tf_op jit(solution)/shard_map/ppermute | solution.py:306
  26.3 6.7 %collective-permute-start.7 = (f32[24,128]{1,0:T(8,128)S(1)}, f32[24,128]{1,0:T(8,128)S(1)}, u32[]{:S(2)}, u32[]{:S(2)}) collective-permute-start(f32[24,128]{1,0:T(8,128)S(1)} %add_add_fusion.2), channel_id=1, source_target_pairs={{0,14},{1,15},{2,4},{3,5},{4,2},{5,3},{6,8},{7,9},{8,6},{9,7},{10,... | collective-permute-start | bytes 36872 | tf_op jit(solution)/shard_map/ppermute | solution.py:306
  33.0 5.5 %collective-permute-start.8 = (f32[24,128]{1,0:T(8,128)S(1)}, f32[24,128]{1,0:T(8,128)S(1)}, u32[]{:S(2)}, u32[]{:S(2)}) collective-permute-start(f32[24,128]{1,0:T(8,128)S(1)} %add.62), channel_id=1, source_target_pairs={{0,6},{1,7},{2,12},{3,13},{4,10},{5,11},{6,0},{7,1},{8,14},{9,15},... | collective-permute-start | bytes 36872 | tf_op jit(solution)/shard_map/ppermute | solution.py:306
  38.5 4.6 %collective-permute-start.11 = (f32[24,128]{1,0:T(8,128)S(1)}, f32[24,128]{1,0:T(8,128)S(1)}, u32[]{:S(2)}, u32[]{:S(2)}) collective-permute-start(f32[24,128]{1,0:T(8,128)S(1)} %add.63), channel_id=1, source_target_pairs={{0,80},{16,64},{32,112},{48,96},{64,16},{80,0},{96,48},{112,32},{1... | collective-permute-start | bytes 36872 | tf_op jit(solution)/shard_map/ppermute | solution.py:306
  38.5 4.6 %collective-permute-start.10 = (f32[24,128]{1,0:T(8,128)S(1)}, f32[24,128]{1,0:T(8,128)S(1)}, u32[]{:S(2)}, u32[]{:S(2)}) collective-permute-start(f32[24,128]{1,0:T(8,128)S(1)} %add.63), channel_id=1, source_target_pairs={{0,64},{16,80},{32,96},{48,112},{64,0},{80,16},{96,32},{112,48},{1... | collective-permute-start | bytes 36872 | tf_op jit(solution)/shard_map/ppermute | solution.py:306
  39.5 4.2 %collective-permute-start.9 = (f32[24,128]{1,0:T(8,128)S(1)}, f32[24,128]{1,0:T(8,128)S(1)}, u32[]{:S(2)}, u32[]{:S(2)}) collective-permute-start(f32[24,128]{1,0:T(8,128)S(1)} %add.63), channel_id=1, source_target_pairs={{0,16},{16,0},{32,48},{48,32},{64,80},{80,64},{96,112},{112,96},{1... | collective-permute-start | bytes 36872 | tf_op jit(solution)/shard_map/ppermute | solution.py:306
  43.7 7.0 %collective-permute-start.14 = (f32[24,128]{1,0:T(8,128)S(1)}, f32[24,128]{1,0:T(8,128)S(1)}, u32[]{:S(2)}, u32[]{:S(2)}) collective-permute-start(f32[24,128]{1,0:T(8,128)S(1)} %add_add_fusion.1), channel_id=1, source_target_pairs={{0,240},{16,224},{32,208},{48,192},{64,176},{80,160},{96,144},{112... | collective-permute-start | bytes 36872 | tf_op jit(solution)/shard_map/ppermute | solution.py:306
  45.8 5.7 %collective-permute-start.13 = (f32[24,128]{1,0:T(8,128)S(1)}, f32[24,128]{1,0:T(8,128)S(1)}, u32[]{:S(2)}, u32[]{:S(2)}) collective-permute-start(f32[24,128]{1,0:T(8,128)S(1)} %add_add_fusion.1), channel_id=1, source_target_pairs={{0,192},{16,208},{32,224},{48,240},{64,128},{80,144},{96,160},{112... | collective-permute-start | bytes 36872 | tf_op jit(solution)/shard_map/ppermute | solution.py:306
  49.7 4.9 %collective-permute-start.12 = (f32[24,128]{1,0:T(8,128)S(1)}, f32[24,128]{1,0:T(8,128)S(1)}, u32[]{:S(2)}, u32[]{:S(2)}) collective-permute-start(f32[24,128]{1,0:T(8,128)S(1)} %add_add_fusion.1), channel_id=1, source_target_pairs={{0,48},{16,32},{32,16},{48,0},{64,112},{80,96},{96,80},{112,64},{1... | collective-permute-start | bytes 36872 | tf_op jit(solution)/shard_map/ppermute | solution.py:306
where the time goes:
time: 66 us; the launch traced here: 65.9 us
  starting transfers between devices  26.5 us (40%)
  waiting for transfers between devices  17 us (26%)
  Pallas kernels  16.9 us (26%)
  matrix products  1.66 us (3%)
  local copies, waits for them, and re-layouts  1.63 us (2%)
  other arithmetic  1.29 us (2%)
  between operations  0.93 us (1%)
    ppermute x11, starting transfers between devices, exchanged(): return lax.ppermute(value, axis, [(i, partner(i)) for i in range(16)])  21.6 us
    ppermute x11, waiting for transfers between devices, exchanged(): return lax.ppermute(value, axis, [(i, partner(i)) for i in range(16)])  14.8 us
    pallas_call x1, Pallas kernels, local(): pl.pallas_call(finish_kernel, in_specs=[vmem] * 6, out_specs=pl.BlockSpec...  11.1 us
    pallas_call x1, Pallas kernels, window(): pl.pallas_call(window_kernel, out_shape=(jax.ShapeDtypeStruct((3, rows, c...  5.03 us
    ppermute x2, starting transfers between devices, window(): lax.ppermute(packed, 'gx', pairs(offset, True))  4.11 us
    ppermute x2, waiting for transfers between devices, window(): lax.ppermute(packed, 'gx', pairs(offset, True))  1.68 us
    dot_general x1, matrix products, window(): lax.dot_general(turned, turned, (((0, 2), (0, 2)), ((), ())), preferred_e...  1.66 us
    transpose x1, local copies, waits for them, and re-layouts, window(): turned = jnp.transpose(basis, (1, 2, 0, 3)).reshape(3 * rows, RANK, cols)  1.6 us
  transfers between devices with their start and end apart: 15, of which 11 were waited for; matrix products, arithmetic and copies ran while one was open for 5% of the time, Pallas kernels for 1%

commit v1 on v0

--- a/solution.py
+++ b/solution.py
@@ -314,13 +314,13 @@
 
 
 def total_over_devices(value):
+    value = quad_sum(value, "gx", 1, 4)
+    value = quad_sum(value, "gx", 3, 12)
     value = quad_sum(value, "gy", 1, 2)
     ring = lambda a: ((a - 1) ^ 1) + 1 if 0 < a < 7 else 7 - a
     value = value + exchanged(value, "gy", lambda i: ring(i // 2) * 2 + i % 2)
     ring = lambda a: (7 - a) if a in (1, 2, 5, 6) else {0: 3, 3: 0, 4: 7, 7: 4}[a]
-    value = value + exchanged(value, "gy", lambda i: ring(i // 2) * 2 + i % 2)
-    value = quad_sum(value, "gx", 1, 4)
-    return quad_sum(value, "gx", 3, 12)
+    return value + exchanged(value, "gy", lambda i: ring(i // 2) * 2 + i % 2)
 
 
 ORDERS = ((0, 0), (0, 1), (1, 0), (0, 2), (1, 1), (2, 0))

time: 66 us -> 65 us (0.985)
  waiting for transfers between devices: 17 us -> 14.5 us
  starting transfers between devices: 26.5 us -> 27.9 us
    ppermute x11, waiting for transfers between devices: 14.8 us -> 12.3 us  [exchanged(): return lax.ppermute(value, axis, [(i, partner(i)) for i in range(16)])]
    ppermute x11, starting transfers between devices: 21.6 us -> 23.1 us  [exchanged(): return lax.ppermute(value, axis, [(i, partner(i)) for i in range(16)])]
  transfers between devices with their start and end apart: 15 -> 15, of which waited for: 11 -> 10; matrix products, arithmetic and copies ran while one was open for 5% -> 5% of each run, Pallas kernels for 1% -> 1%
where the time goes in v1:
time: 65 us; the launch traced here: 64.8 us
  starting transfers between devices  27.9 us (43%)
  Pallas kernels  16.9 us (26%)
  waiting for transfers between devices  14.5 us (22%)
  matrix products  1.66 us (3%)
  local copies, waits for them, and re-layouts  1.63 us (3%)
  other arithmetic  1.29 us (2%)
  between operations  0.93 us (1%)
    ppermute x11, starting transfers between devices, exchanged(): return lax.ppermute(value, axis, [(i, partner(i)) for i in range(16)])  23.1 us
    ppermute x11, waiting for transfers between devices, exchanged(): return lax.ppermute(value, axis, [(i, partner(i)) for i in range(16)])  12.3 us
    pallas_call x1, Pallas kernels, local(): pl.pallas_call(finish_kernel, in_specs=[vmem] * 6, out_specs=pl.BlockSpec...  11.1 us
    pallas_call x1, Pallas kernels, window(): pl.pallas_call(window_kernel, out_shape=(jax.ShapeDtypeStruct((3, rows, c...  5.03 us
    ppermute x2, starting transfers between devices, window(): lax.ppermute(packed, 'gx', pairs(offset, True))  4.11 us
    ppermute x2, waiting for transfers between devices, window(): lax.ppermute(packed, 'gx', pairs(offset, True))  1.68 us
    dot_general x1, matrix products, window(): lax.dot_general(turned, turned, (((0, 2), (0, 2)), ((), ())), preferred_e...  1.66 us
    transpose x1, local copies, waits for them, and re-layouts, window(): turned = jnp.transpose(basis, (1, 2, 0, 3)).reshape(3 * rows, RANK, cols)  1.6 us
  transfers between devices with their start and end apart: 15, of which 10 were waited for; matrix products, arithmetic and copies ran while one was open for 5% of the time, Pallas kernels for 1%

profile of v1, /device:TPU:6, one launch (start us, length us, event | category | flops | bytes accessed | tf_op | source)
XLA Modules:
  0.0 64.8 jit_solution(4705815934770110481)
XLA Ops:
  0.6 0.0 copy-start
  0.6 1.2 %pad_add_fusion.fields.fields_low.fields_high = f32[6,120,128]{2,1,0:T(8,128)S(1)} fusion(f32[1,120,128]{2,1,0:T(8,128)} %bitcast.16, s32[1,120,128]{2,1,0:T(8,128)} %bitcast.17, f32[1,120,128]{2,1,0:T(8,128)} %bitcast.18, f32[3,120,128]{2,1,0:T(8,128)} %param.7), kind=kLoop, calls=%fused_computation.1 | loop fusion | flops 368640 | bytes 737280 | tf_op jit(solution)/shard_map/add | solution.py:255
  1.8 0.1 shard_map.86
  2.0 1.7 %collective-permute-start = (f32[120,128]{1,0:T(8,128)S(1)}, f32[120,128]{1,0:T(8,128)S(1)}, u32[]{:S(2)}, u32[]{:S(2)}) collective-permute-start(f32[120,128]{1,0:T(8,128)S(1)} %shard_map.86), channel_id=1, source_target_pairs={{0,16},{16,0},{32,48},{48,32},{64,80},{80,64},{96,112},{112,96},{1... | collective-permute-start | bytes 184328 | tf_op jit(solution)/shard_map/ppermute | solution.py:262
  3.6 2.4 %collective-permute-start.1 = (f32[120,128]{1,0:T(8,128)S(1)}, f32[120,128]{1,0:T(8,128)S(1)}, u32[]{:S(2)}, u32[]{:S(2)}) collective-permute-start(f32[120,128]{1,0:T(8,128)S(1)} %shard_map.86), channel_id=1, source_target_pairs={{0,240},{16,32},{32,16},{48,64},{64,48},{80,96},{96,80},{112,128},... | collective-permute-start | bytes 184328 | tf_op jit(solution)/shard_map/ppermute | solution.py:262
  6.1 0.6 shard_map.87.rest_2_
  6.7 0.0 collective-permute-done.first_low.first_high.first_side
  6.7 0.0 copy-done
  6.7 1.6 %copy.9 = bf16[3,120,64,128]{3,2,1,0:T(8,128)(2,1)S(1)} copy(bf16[3,120,64,128]{3,1,0,2:T(8,128)(2,1)S(1)} %bitcast.15) | data formatting | bytes 11796480 | tf_op jit(solution)/shard_map/transpose | solution.py:269
  8.3 1.7 %collective-permute-done.1.second_low.second_high.second_side = f32[120,128]{1,0:T(8,128)S(1)} collective-permute-done((f32[120,128]{1,0:T(8,128)S(1)}, f32[120,128]{1,0:T(8,128)S(1)}, u32[]{:S(2)}, u32[]{:S(2)}) %collective-permute-start.1) | collective-permute-done | bytes 61472 | tf_op jit(solution)/shard_map/ppermute | solution.py:262
  10.0 0.1 collective-permute-start.2
  10.1 0.0 copy-start.1
  10.1 0.7 %collective-permute-start.3 = (f32[80,128]{1,0:T(8,128)S(1)}, f32[80,128]{1,0:T(8,128)S(1)}, u32[]{:S(2)}, u32[]{:S(2)}) collective-permute-start(f32[80,128]{1,0:T(8,128)S(1)} %get-tuple-element.35), channel_id=1, source_target_pairs={{1,2},{2,1},{3,4},{4,3},{5,6},{6,5},{7,8},{8,7},{9,10},{10,9},{11,... | collective-permute-start | bytes 122888 | tf_op jit(solution)/shard_map/ppermute | solution.py:284
  10.8 0.5 collective-permute-done.2.first_rows
  11.3 1.7 %convolution_bitcast_fusion.rest_1_ = f32[64,64]{1,0:T(8,128)S(1)} fusion(bf16[360,64,128]{2,1,0:T(8,128)(2,1)S(1)} %bitcast.12), kind=kOutput, calls=%fused_computation | convolution fusion | flops 377487360 | bytes 5914624 | tf_op jit(solution)/shard_map/dot_general | solution.py:286
  13.0 0.0 copy-start.3
  13.0 0.0 copy-start.2
  13.0 0.0 collective-permute-done.3.second_rows
  13.0 0.0 copy-done.1
  13.0 5.0 %shard_map.90 = (f32[3,120,128]{2,1,0:T(8,128)}, bf16[360,8,128]{2,1,0:T(8,128)(2,1)S(1)}, f32[24,128]{1,0:T(8,128)S(1)}) custom-call(f32[6,120,128]{2,1,0:T(8,128)S(1)} %pad_add_fusion.fields.fields_low.fields_high, f32[120,128]{1,0:T(8,128)S(1)} %collective-permute-done.first_low.first_high.first_side, ...), custom_call_target="tpu_custom_call" | custom-call | tf_op jit(solution)/shard_map/pallas_call | solution.py:291
  18.1 0.0 collective-permute-start.6
  18.1 1.0 %collective-permute-start.5 = (f32[24,128]{1,0:T(8,128)S(1)}, f32[24,128]{1,0:T(8,128)S(1)}, u32[]{:S(2)}, u32[]{:S(2)}) collective-permute-start(f32[24,128]{1,0:T(8,128)S(1)} %get-tuple-element.42), channel_id=1, source_target_pairs={{0,64},{16,80},{32,96},{48,112},{64,0},{80,16},{96,32},{112,48},{1... | collective-permute-start | bytes 36872 | tf_op jit(solution)/shard_map/ppermute | solution.py:306
  19.0 2.5 %collective-permute-start.4 = (f32[24,128]{1,0:T(8,128)S(1)}, f32[24,128]{1,0:T(8,128)S(1)}, u32[]{:S(2)}, u32[]{:S(2)}) collective-permute-start(f32[24,128]{1,0:T(8,128)S(1)} %get-tuple-element.42), channel_id=1, source_target_pairs={{0,16},{16,0},{32,48},{48,32},{64,80},{80,64},{96,112},{112,96},{1... | collective-permute-start | bytes 36872 | tf_op jit(solution)/shard_map/ppermute | solution.py:306
  21.5 1.1 %collective-permute-done.6 = f32[24,128]{1,0:T(8,128)S(1)} collective-permute-done((f32[24,128]{1,0:T(8,128)S(1)}, f32[24,128]{1,0:T(8,128)S(1)}, u32[]{:S(2)}, u32[]{:S(2)}) %collective-permute-start.6) | collective-permute-done | bytes 12320 | tf_op jit(solution)/shard_map/ppermute | solution.py:306
  22.6 0.0 collective-permute-done.5
  22.6 0.6 collective-permute-done.4
  23.2 2.1 %collective-permute-start.9 = (f32[24,128]{1,0:T(8,128)S(1)}, f32[24,128]{1,0:T(8,128)S(1)}, u32[]{:S(2)}, u32[]{:S(2)}) collective-permute-start(f32[24,128]{1,0:T(8,128)S(1)} %add_add_fusion.2), channel_id=1, source_target_pairs={{0,240},{16,224},{32,208},{48,192},{64,176},{80,160},{96,144},{112... | collective-permute-start | bytes 36872 | tf_op jit(solution)/shard_map/ppermute | solution.py:306
  25.3 3.9 %collective-permute-start.8 = (f32[24,128]{1,0:T(8,128)S(1)}, f32[24,128]{1,0:T(8,128)S(1)}, u32[]{:S(2)}, u32[]{:S(2)}) collective-permute-start(f32[24,128]{1,0:T(8,128)S(1)} %add_add_fusion.2), channel_id=1, source_target_pairs={{0,192},{16,208},{32,224},{48,240},{64,128},{80,144},{96,160},{112... | collective-permute-start | bytes 36872 | tf_op jit(solution)/shard_map/ppermute | solution.py:306
  29.3 0.0 collective-permute-start.7
  29.3 0.9 %collective-permute-done.9 = f32[24,128]{1,0:T(8,128)S(1)} collective-permute-done((f32[24,128]{1,0:T(8,128)S(1)}, f32[24,128]{1,0:T(8,128)S(1)}, u32[]{:S(2)}, u32[]{:S(2)}) %collective-permute-start.9) | collective-permute-done | bytes 12320 | tf_op jit(solution)/shard_map/ppermute | solution.py:306
  30.2 0.8 %collective-permute-done.8 = f32[24,128]{1,0:T(8,128)S(1)} collective-permute-done((f32[24,128]{1,0:T(8,128)S(1)}, f32[24,128]{1,0:T(8,128)S(1)}, u32[]{:S(2)}, u32[]{:S(2)}) %collective-permute-start.8) | collective-permute-done | bytes 12320 | tf_op jit(solution)/shard_map/ppermute | solution.py:306
  31.1 3.2 %collective-permute-done.7 = f32[24,128]{1,0:T(8,128)S(1)} collective-permute-done((f32[24,128]{1,0:T(8,128)S(1)}, f32[24,128]{1,0:T(8,128)S(1)}, u32[]{:S(2)}, u32[]{:S(2)}) %collective-permute-start.7) | collective-permute-done | bytes 12320 | tf_op jit(solution)/shard_map/ppermute | solution.py:306
  34.3 1.6 %collective-permute-start.12 = (f32[24,128]{1,0:T(8,128)S(1)}, f32[24,128]{1,0:T(8,128)S(1)}, u32[]{:S(2)}, u32[]{:S(2)}) collective-permute-start(f32[24,128]{1,0:T(8,128)S(1)} %add_add_fusion.1), channel_id=1, source_target_pairs={{0,3},{1,2},{2,1},{3,0},{4,7},{5,6},{6,5},{7,4},{8,11},{9,10},{10,... | collective-permute-start | bytes 36872 | tf_op jit(solution)/shard_map/ppermute | solution.py:306
  35.9 2.7 %collective-permute-start.11 = (f32[24,128]{1,0:T(8,128)S(1)}, f32[24,128]{1,0:T(8,128)S(1)}, u32[]{:S(2)}, u32[]{:S(2)}) collective-permute-start(f32[24,128]{1,0:T(8,128)S(1)} %add_add_fusion.1), channel_id=1, source_target_pairs={{0,2},{1,3},{2,0},{3,1},{4,6},{5,7},{6,4},{7,5},{8,10},{9,11},{10,... | collective-permute-start | bytes 36872 | tf_op jit(solution)/shard_map/ppermute | solution.py:306
  38.6 0.0 collective-permute-start.10
  38.6 0.0 collective-permute-done.12
  38.7 1.7 %collective-permute-done.11 = f32[24,128]{1,0:T(8,128)S(1)} collective-permute-done((f32[24,128]{1,0:T(8,128)S(1)}, f32[24,128]{1,0:T(8,128)S(1)}, u32[]{:S(2)}, u32[]{:S(2)}) %collective-permute-start.11) | collective-permute-done | bytes 12320 | tf_op jit(solution)/shard_map/ppermute | solution.py:306
  40.3 0.0 collective-permute-done.10
  40.3 6.1 %collective-permute-start.13 = (f32[24,128]{1,0:T(8,128)S(1)}, f32[24,128]{1,0:T(8,128)S(1)}, u32[]{:S(2)}, u32[]{:S(2)}) collective-permute-start(f32[24,128]{1,0:T(8,128)S(1)} %add_add_fusion), channel_id=1, source_target_pairs={{0,14},{1,15},{2,4},{3,5},{4,2},{5,3},{6,8},{7,9},{8,6},{9,7},{10,... | collective-permute-start | bytes 36872 | tf_op jit(solution)/shard_map/ppermute | solution.py:306
  46.4 0.0 copy-done.3
  46.4 1.7 %collective-permute-done.13 = f32[24,128]{1,0:T(8,128)S(1)} collective-permute-done((f32[24,128]{1,0:T(8,128)S(1)}, f32[24,128]{1,0:T(8,128)S(1)}, u32[]{:S(2)}, u32[]{:S(2)}) %collective-permute-start.13) | collective-permute-done | bytes 12320 | tf_op jit(solution)/shard_map/ppermute | solution.py:306
  48.1 3.0 %collective-permute-start.14 = (f32[24,128]{1,0:T(8,128)S(1)}, f32[24,128]{1,0:T(8,128)S(1)}, u32[]{:S(2)}, u32[]{:S(2)}) collective-permute-start(f32[24,128]{1,0:T(8,128)S(1)} %add.68), channel_id=1, source_target_pairs={{0,6},{1,7},{2,12},{3,13},{4,10},{5,11},{6,0},{7,1},{8,14},{9,15},... | collective-permute-start | bytes 36872 | tf_op jit(solution)/shard_map/ppermute | solution.py:306
  51.1 0.1 multiply_multiply_fusion.outer
  51.2 0.0 copy-done.2
  51.3 2.3 %collective-permute-done.14 = f32[24,128]{1,0:T(8,128)S(1)} collective-permute-done((f32[24,128]{1,0:T(8,128)S(1)}, f32[24,128]{1,0:T(8,128)S(1)}, u32[]{:S(2)}, u32[]{:S(2)}) %collective-permute-start.14) | collective-permute-done | bytes 12320 | tf_op jit(solution)/shard_map/ppermute | solution.py:306
  53.6 11.1 %shard_map.91 = bf16[64,3,120,128]{3,2,1,0:T(8,128)(2,1)} custom-call(f32[24,128]{1,0:T(8,128)S(1)} %add.69.sums, f32[128,128]{1,0:T(8,128)S(1)} %multiply_multiply_fusion.outer, f32[64,128]{1,0:T(8,128)S(1)} %pad.30.start, f32[1,128]{1,0:T(1,128)S(1)} %get-tuple-element.44.weights, bf16[360,8,128]{2,1,0:T(8,128)(2,1)S(1)} %get-tuple-element.43.snaps, ...), custom_call_target="tpu_custom_call" | custom-call | tf_op jit(solution)/shard_map/pallas_call | solution.py:465
  (9 shorter events, 0.1 us)
Async XLA Ops:
  0.6 6.1 %copy-start = (bf16[64,3,120,128]{3,2,1,0:T(8,128)(2,1)S(1)}, bf16[64,3,120,128]{3,2,1,0:T(8,128)(2,1)}, u32[]{:S(2)}) copy-start(bf16[64,3,120,128]{3,2,1,0:T(8,128)(2,1)} %value.1) | copy-start | bytes 17694724
  2.0 4.7 %collective-permute-start = (f32[120,128]{1,0:T(8,128)S(1)}, f32[120,128]{1,0:T(8,128)S(1)}, u32[]{:S(2)}, u32[]{:S(2)}) collective-permute-start(f32[120,128]{1,0:T(8,128)S(1)} %shard_map.86), channel_id=1, source_target_pairs={{0,16},{16,0},{32,48},{48,32},{64,80},{80,64},{96,112},{112,96},{1... | collective-permute-start | bytes 184328 | tf_op jit(solution)/shard_map/ppermute | solution.py:262
  3.6 6.3 %collective-permute-start.1 = (f32[120,128]{1,0:T(8,128)S(1)}, f32[120,128]{1,0:T(8,128)S(1)}, u32[]{:S(2)}, u32[]{:S(2)}) collective-permute-start(f32[120,128]{1,0:T(8,128)S(1)} %shard_map.86), channel_id=1, source_target_pairs={{0,240},{16,32},{32,16},{48,64},{64,48},{80,96},{96,80},{112,128},... | collective-permute-start | bytes 184328 | tf_op jit(solution)/shard_map/ppermute | solution.py:262
  10.0 1.3 %collective-permute-start.2 = (f32[80,128]{1,0:T(8,128)S(1)}, f32[80,128]{1,0:T(8,128)S(1)}, u32[]{:S(2)}, u32[]{:S(2)}) collective-permute-start(f32[80,128]{1,0:T(8,128)S(1)} %get-tuple-element.32), channel_id=1, source_target_pairs={{0,1},{1,0},{2,3},{3,2},{4,5},{5,4},{6,7},{7,6},{8,9},{9,8},{10,11... | collective-permute-start | bytes 122888 | tf_op jit(solution)/shard_map/ppermute | solution.py:284
  10.1 2.9 %copy-start.1 = (f32[8,128]{1,0:T(8,128)S(1)}, f32[8,128]{1,0:T(8,128)}, u32[]{:S(2)}) copy-start(f32[8,128]{1,0:T(8,128)} %shard_map.87.rest_2_) | copy-start | bytes 12292
  10.1 2.9 %collective-permute-start.3 = (f32[80,128]{1,0:T(8,128)S(1)}, f32[80,128]{1,0:T(8,128)S(1)}, u32[]{:S(2)}, u32[]{:S(2)}) collective-permute-start(f32[80,128]{1,0:T(8,128)S(1)} %get-tuple-element.35), channel_id=1, source_target_pairs={{1,2},{2,1},{3,4},{4,3},{5,6},{6,5},{7,8},{8,7},{9,10},{10,9},{11,... | collective-permute-start | bytes 122888 | tf_op jit(solution)/shard_map/ppermute | solution.py:284
  13.0 33.4 %copy-start.3 = (f32[64]{0:T(128)S(1)}, f32[64]{0:T(128)}, u32[]{:S(2)}) copy-start(f32[64]{0:T(128)} %param.12) | copy-start | bytes 772
  13.0 38.2 %copy-start.2 = (f32[68,64]{0,1:T(8,128)S(1)}, f32[68,64]{0,1:T(8,128)}, u32[]{:S(2)}) copy-start(f32[68,64]{0,1:T(8,128)} %param.13) | copy-start | bytes 52228
  18.1 4.6 %collective-permute-start.6 = (f32[24,128]{1,0:T(8,128)S(1)}, f32[24,128]{1,0:T(8,128)S(1)}, u32[]{:S(2)}, u32[]{:S(2)}) collective-permute-start(f32[24,128]{1,0:T(8,128)S(1)} %get-tuple-element.42), channel_id=1, source_target_pairs={{0,80},{16,64},{32,112},{48,96},{64,16},{80,0},{96,48},{112,32},{1... | collective-permute-start | bytes 36872 | tf_op jit(solution)/shard_map/ppermute | solution.py:306
  18.1 4.6 %collective-permute-start.5 = (f32[24,128]{1,0:T(8,128)S(1)}, f32[24,128]{1,0:T(8,128)S(1)}, u32[]{:S(2)}, u32[]{:S(2)}) collective-permute-start(f32[24,128]{1,0:T(8,128)S(1)} %get-tuple-element.42), channel_id=1, source_target_pairs={{0,64},{16,80},{32,96},{48,112},{64,0},{80,16},{96,32},{112,48},{1... | collective-permute-start | bytes 36872 | tf_op jit(solution)/shard_map/ppermute | solution.py:306
  19.0 4.2 %collective-permute-start.4 = (f32[24,128]{1,0:T(8,128)S(1)}, f32[24,128]{1,0:T(8,128)S(1)}, u32[]{:S(2)}, u32[]{:S(2)}) collective-permute-start(f32[24,128]{1,0:T(8,128)S(1)} %get-tuple-element.42), channel_id=1, source_target_pairs={{0,16},{16,0},{32,48},{48,32},{64,80},{80,64},{96,112},{112,96},{1... | collective-permute-start | bytes 36872 | tf_op jit(solution)/shard_map/ppermute | solution.py:306
  23.2 7.0 %collective-permute-start.9 = (f32[24,128]{1,0:T(8,128)S(1)}, f32[24,128]{1,0:T(8,128)S(1)}, u32[]{:S(2)}, u32[]{:S(2)}) collective-permute-start(f32[24,128]{1,0:T(8,128)S(1)} %add_add_fusion.2), channel_id=1, source_target_pairs={{0,240},{16,224},{32,208},{48,192},{64,176},{80,160},{96,144},{112... | collective-permute-start | bytes 36872 | tf_op jit(solution)/shard_map/ppermute | solution.py:306
  25.3 5.7 %collective-permute-start.8 = (f32[24,128]{1,0:T(8,128)S(1)}, f32[24,128]{1,0:T(8,128)S(1)}, u32[]{:S(2)}, u32[]{:S(2)}) collective-permute-start(f32[24,128]{1,0:T(8,128)S(1)} %add_add_fusion.2), channel_id=1, source_target_pairs={{0,192},{16,208},{32,224},{48,240},{64,128},{80,144},{96,160},{112... | collective-permute-start | bytes 36872 | tf_op jit(solution)/shard_map/ppermute | solution.py:306
  29.3 5.0 %collective-permute-start.7 = (f32[24,128]{1,0:T(8,128)S(1)}, f32[24,128]{1,0:T(8,128)S(1)}, u32[]{:S(2)}, u32[]{:S(2)}) collective-permute-start(f32[24,128]{1,0:T(8,128)S(1)} %add_add_fusion.2), channel_id=1, source_target_pairs={{0,48},{16,32},{32,16},{48,0},{64,112},{80,96},{96,80},{112,64},{1... | collective-permute-start | bytes 36872 | tf_op jit(solution)/shard_map/ppermute | solution.py:306
  34.3 4.4 %collective-permute-start.12 = (f32[24,128]{1,0:T(8,128)S(1)}, f32[24,128]{1,0:T(8,128)S(1)}, u32[]{:S(2)}, u32[]{:S(2)}) collective-permute-start(f32[24,128]{1,0:T(8,128)S(1)} %add_add_fusion.1), channel_id=1, source_target_pairs={{0,3},{1,2},{2,1},{3,0},{4,7},{5,6},{6,5},{7,4},{8,11},{9,10},{10,... | collective-permute-start | bytes 36872 | tf_op jit(solution)/shard_map/ppermute | solution.py:306
  35.9 4.4 %collective-permute-start.11 = (f32[24,128]{1,0:T(8,128)S(1)}, f32[24,128]{1,0:T(8,128)S(1)}, u32[]{:S(2)}, u32[]{:S(2)}) collective-permute-start(f32[24,128]{1,0:T(8,128)S(1)} %add_add_fusion.1), channel_id=1, source_target_pairs={{0,2},{1,3},{2,0},{3,1},{4,6},{5,7},{6,4},{7,5},{8,10},{9,11},{10,... | collective-permute-start | bytes 36872 | tf_op jit(solution)/shard_map/ppermute | solution.py:306
  38.6 1.7 %collective-permute-start.10 = (f32[24,128]{1,0:T(8,128)S(1)}, f32[24,128]{1,0:T(8,128)S(1)}, u32[]{:S(2)}, u32[]{:S(2)}) collective-permute-start(f32[24,128]{1,0:T(8,128)S(1)} %add_add_fusion.1), channel_id=1, source_target_pairs={{0,1},{1,0},{2,3},{3,2},{4,5},{5,4},{6,7},{7,6},{8,9},{9,8},{10,11... | collective-permute-start | bytes 36872 | tf_op jit(solution)/shard_map/ppermute | solution.py:306
  40.3 7.7 %collective-permute-start.13 = (f32[24,128]{1,0:T(8,128)S(1)}, f32[24,128]{1,0:T(8,128)S(1)}, u32[]{:S(2)}, u32[]{:S(2)}) collective-permute-start(f32[24,128]{1,0:T(8,128)S(1)} %add_add_fusion), channel_id=1, source_target_pairs={{0,14},{1,15},{2,4},{3,5},{4,2},{5,3},{6,8},{7,9},{8,6},{9,7},{10,... | collective-permute-start | bytes 36872 | tf_op jit(solution)/shard_map/ppermute | solution.py:306
  48.1 5.5 %collective-permute-start.14 = (f32[24,128]{1,0:T(8,128)S(1)}, f32[24,128]{1,0:T(8,128)S(1)}, u32[]{:S(2)}, u32[]{:S(2)}) collective-permute-start(f32[24,128]{1,0:T(8,128)S(1)} %add.68), channel_id=1, source_target_pairs={{0,6},{1,7},{2,12},{3,13},{4,10},{5,11},{6,0},{7,1},{8,14},{9,15},... | collective-permute-start | bytes 36872 | tf_op jit(solution)/shard_map/ppermute | solution.py:306
